TPU v7x, 256 devices: a whole 4x4x8 slice. The times are simulated.
256 devices in a mesh: box: 64 (over x, z, core), cone: 4 (over y).
Axes of the slice: x: 4, y: 4, z: 8, core: 2. Of those that a mesh axis runs over, the one named last changes fastest.
Arguments:
- mom_current: bfloat16 [16384, 512], P('box'), may hold values from -6 to 6
- mom_radiate: bfloat16 [8, 512, 512], P('cone'), may hold values from -0.25 to 0.25
- po_receive: bfloat16 [8, 512, 512], P('cone'), may hold values from -0.09375 to 0.09375
- po_radiate: bfloat16 [8, 512, 512], P('cone'), may hold values from -0.25 to 0.25
- mom_receive: bfloat16 [8, 512, 512], P('cone'), may hold values from -0.03125 to 0.03125
- dirs: float32 [8, 3, 256], P('cone'), may hold values from -4 to 4
- mom_center: float32 [3, 16384], replicated, may hold values from 0 to 4
- po_center: float32 [3, 32768], replicated, may hold values from 0 to 4
- po_src: int32 [8, 32768], P(None, 'box'), may hold values from 0 to 16383, as said below
- po_weight: float32 [8, 32768], P(None, 'box'), may hold values from 0.2 to 2
- mom_src: int32 [8, 16384], P(None, 'box'), may hold values from 0 to 32767, as said below
- mom_weight: float32 [8, 16384], P(None, 'box'), may hold values from 0.2 to 2
- lit: int32 [8, 32768], P('cone', 'box'), may hold values 0 or 1
Outputs:
- mom_field: float32 [16384, 512], P('box', 'cone')
- po_current: bfloat16 [32768, 512], P('box', 'cone')
Inputs may be any that keep to these rules, and one draw needn't show every extreme that they name: |po_src[l, q] - q * 256 // 512| <= 256 for every entry. |mom_src[l, m] - m * 2| <= 512 for every entry.
All inputs are finite; a program needn't handle non-finite values. No bound on the sum of `lit` on one device may be relied on, other than what follows from the above.
Results may differ from a plain program's by a relative error of at most 0.0085.
Values may be sent and summed in bfloat16 or wider, within the bound.
No kernel may reach another device: no remote copies, remote signals or barrier semaphores. Data moves between devices by JAX's collectives and lax.ppermute only.
A program may use at most 64 MiB of HBM per device.

v0:
```python
import jax
import jax.numpy as jnp
from jax import lax
from jax.sharding import PartitionSpec as P


def padded_2(shard, sides, width):
    for axis, dim in sides:
        size, length = (lax.axis_size(axis), shard.shape[dim])
        up = [(i, (i + 1) % size) for i in range(size - 1)]
        down = [(j, i) for i, j in up]
        last = lax.slice_in_dim(shard, length - width, length, axis=dim)
        leading = lax.slice_in_dim(shard, 0, width, axis=dim)
        before = lax.ppermute(last, axis, up)
        after = lax.ppermute(leading, axis, down)
        shard = jnp.concatenate([before, shard, after], axis=dim)
    return shard


def phases(dirs, centers):
    return (
        centers[0][:, None, None] * dirs[None, :, 0, :]
        + centers[1][:, None, None] * dirs[None, :, 1, :]
        + centers[2][:, None, None] * dirs[None, :, 2, :]
    )


def rotate(waves, theta, orient):
    samples = theta.shape[-1]
    real_part = waves[..., :samples]
    imag_part = waves[..., samples:]
    cosine = jnp.cos(theta)
    sine = orient * jnp.sin(theta)
    return jnp.concatenate(
        [real_part * cosine - imag_part * sine, real_part * sine + imag_part * cosine], axis=-1
    )


def collect(padded, sources, weights, offset):
    rows_all, cone_count, width = padded.shape
    flat = padded.reshape(rows_all, cone_count * width)
    total = jnp.zeros((sources.shape[1], cone_count * width), jnp.float32)
    for slot in range(sources.shape[0]):
        picked = jnp.take(flat, sources[slot] - offset, axis=0).astype(jnp.float32)
        total = total + weights[slot][:, None] * picked
    return total.reshape(sources.shape[1], cone_count, width)


def shards(
    mom_current,
    mom_radiate,
    po_receive,
    po_radiate,
    mom_receive,
    dirs,
    mom_center,
    po_center,
    po_src,
    po_weight,
    mom_src,
    mom_weight,
    lit,
):
    box_index = lax.axis_index("box")
    mom_rows = mom_current.shape[0]
    po_rows = lit.shape[1]
    mom_theta = phases(
        dirs, lax.dynamic_slice_in_dim(mom_center, box_index * mom_rows, mom_rows, 1)
    )
    po_theta = phases(dirs, lax.dynamic_slice_in_dim(po_center, box_index * po_rows, po_rows, 1))
    radiated = jnp.einsum(
        "rn,cnk->rck", mom_current, mom_radiate, preferred_element_type=jnp.float32
    )
    mom_waves = rotate(radiated, mom_theta, -1.0).astype(jnp.bfloat16)
    mom_padded = padded_2(mom_waves, (("box", 0),), mom_rows)
    gathered = collect(mom_padded, po_src, po_weight, (box_index - 1) * mom_rows)
    lit_rows = jnp.transpose(lit).astype(jnp.float32)
    po_lit = (rotate(gathered, po_theta, 1.0) * lit_rows[:, :, None]).astype(jnp.bfloat16)
    partial_value = jnp.einsum(
        "rck,ckn->rn", po_lit, po_receive, preferred_element_type=jnp.float32
    )
    po_whole = lax.psum(partial_value, "cone").astype(jnp.bfloat16)
    share = po_whole.shape[1] // lax.axis_size("cone")
    po_share = lax.dynamic_slice_in_dim(po_whole, lax.axis_index("cone") * share, share, 1)
    radiated = jnp.einsum("rn,cnk->rck", po_whole, po_radiate, preferred_element_type=jnp.float32)
    po_waves = rotate(radiated, po_theta, -1.0).astype(jnp.bfloat16)
    po_padded = padded_2(po_waves, (("box", 0),), po_rows)
    returned = collect(po_padded, mom_src, mom_weight, (box_index - 1) * po_rows)
    mom_incident = rotate(returned, mom_theta, 1.0).astype(jnp.bfloat16)
    mom_partial = jnp.einsum(
        "rck,ckn->rn", mom_incident, mom_receive, preferred_element_type=jnp.float32
    )
    mom_field = lax.psum_scatter(mom_partial, "cone", scatter_dimension=1, tiled=True)
    return (mom_field, po_share)


def solution(mesh):
    in_specs = (
        P("box", None),
        P("cone", None, None),
        P("cone", None, None),
        P("cone", None, None),
        P("cone", None, None),
        P("cone", None, None),
        P(),
        P(),
        P(None, "box"),
        P(None, "box"),
        P(None, "box"),
        P(None, "box"),
        P("cone", "box"),
    )
    out_specs = (P("box", "cone"), P("box", "cone"))
    return jax.shard_map(shards, mesh=mesh, in_specs=in_specs, out_specs=out_specs, check_vma=False)
```

profile of v0, /device:TPU:2, one launch (start us, length us, event | category | flops | bytes accessed | tf_op | source)
XLA Modules:
  0.0 210.0 jit_solution(1306298672080685042)
XLA Ops:
  10.7 2.5 %subtract_convert_fusion.2 = (bf16[256,2,256]{2,0,1:T(8,128)(2,1)S(1)}, bf16[256,2,256]{2,0,1:T(8,128)(2,1)S(1)}) fusion(f32[256,2,512]{2,0,1:T(8,128)S(1)} %fusion.14, f32[2,256]{1,0:T(2,128)S(1)} %get-tuple-element.53, f32[256]{0:T(256)S(1)} %bitcast.110, f32[2,256]{1,0:T(2,128)S(1)} %get-tuple-element.54, f32[256]{0:T(256)S(1)} %bitcast.108, ...), kind=kLoop, calls=%fused_computation.43 | loop fusion | flops 1835008 | bytes 1582080 | tf_op jit(solution)/shard_map/convert.4
  13.3 1.9 collective-permute-start
  15.2 7.2 %collective-permute-start.1 = (bf16[256,2,512]{2,0,1:T(8,128)(2,1)S(1)}, bf16[256,2,512]{2,0,1:T(8,128)(2,1)}, u32[]{:S(2)}, u32[]{:S(2)}) collective-permute-start(bf16[256,2,512]{2,0,1:T(8,128)(2,1)S(1)} %pad_maximum_fusion.3), channel_id=1, source_target_pairs={{4,0},{8,4},{12,8},{16,12},{20,16},{24,20},{28,24},{32,28},{36,32}... | collective-permute-start | bytes 1572872 | tf_op jit(solution)/shard_map/ppermute | solution.py:15
  23.8 3.5 %collective-permute-done = bf16[256,2,512]{2,0,1:T(8,128)(2,1)S(1)} collective-permute-done((bf16[256,2,512]{2,0,1:T(8,128)(2,1)S(1)}, bf16[256,2,512]{2,0,1:T(8,128)(2,1)S(1)}, u32[]{:S(2)}, u32[]{:S(2)}) %collective-permute-start) | collective-permute-done | bytes 524320 | tf_op jit(solution)/shard_map/ppermute | solution.py:14
  33.7 2.8 %gather_fusion = bf16[512,1024]{1,0:T(8,128)(2,1)} fusion(bf16[768,1024]{1,0:T(8,128)(2,1)S(1)} %copy.27, s32[1024]{0:T(1024)S(1)} %pad_clamp_fusion.15), kind=kCustom, calls=%fused_computation.clone | custom fusion | bytes 2099200 | tf_op jit(solution)/shard_map/jit(_take)/gather | solution.py:44
  36.5 2.8 %gather_fusion.1 = bf16[512,1024]{1,0:T(8,128)(2,1)} fusion(bf16[768,1024]{1,0:T(8,128)(2,1)S(1)} %copy.27, s32[1024]{0:T(1024)S(1)} %pad_clamp_fusion.14), kind=kCustom, calls=%fused_computation.2.clone | custom fusion | bytes 2099200 | tf_op jit(solution)/shard_map/jit(_take)/gather | solution.py:44
  39.3 2.8 %gather_fusion.2 = bf16[512,1024]{1,0:T(8,128)(2,1)} fusion(bf16[768,1024]{1,0:T(8,128)(2,1)S(1)} %copy.27, s32[1024]{0:T(1024)S(1)} %pad_clamp_fusion.13), kind=kCustom, calls=%fused_computation.3.clone | custom fusion | bytes 2099200 | tf_op jit(solution)/shard_map/jit(_take)/gather | solution.py:44
  42.1 2.8 %gather_fusion.3 = bf16[512,1024]{1,0:T(8,128)(2,1)} fusion(bf16[768,1024]{1,0:T(8,128)(2,1)S(1)} %copy.27, s32[1024]{0:T(1024)S(1)} %pad_clamp_fusion.12), kind=kCustom, calls=%fused_computation.4.clone | custom fusion | bytes 2099200 | tf_op jit(solution)/shard_map/jit(_take)/gather | solution.py:44
  44.9 2.8 %gather_fusion.4 = bf16[512,1024]{1,0:T(8,128)(2,1)} fusion(bf16[768,1024]{1,0:T(8,128)(2,1)S(1)} %copy.27, s32[1024]{0:T(1024)S(1)} %pad_clamp_fusion.11), kind=kCustom, calls=%fused_computation.5.clone | custom fusion | bytes 2099200 | tf_op jit(solution)/shard_map/jit(_take)/gather | solution.py:44
  47.6 2.8 %gather_fusion.5 = bf16[512,1024]{1,0:T(8,128)(2,1)} fusion(bf16[768,1024]{1,0:T(8,128)(2,1)S(1)} %copy.27, s32[1024]{0:T(1024)S(1)} %pad_clamp_fusion.10), kind=kCustom, calls=%fused_computation.6.clone | custom fusion | bytes 2099200 | tf_op jit(solution)/shard_map/jit(_take)/gather | solution.py:44
  50.4 2.8 %gather_fusion.6 = bf16[512,1024]{1,0:T(8,128)(2,1)} fusion(bf16[768,1024]{1,0:T(8,128)(2,1)S(1)} %copy.27, s32[1024]{0:T(1024)S(1)} %pad_clamp_fusion.9), kind=kCustom, calls=%fused_computation.7.clone | custom fusion | bytes 2099200 | tf_op jit(solution)/shard_map/jit(_take)/gather | solution.py:44
  53.1 2.8 %gather_fusion.7 = bf16[512,1024]{1,0:T(8,128)(2,1)} fusion(bf16[768,1024]{1,0:T(8,128)(2,1)S(1)} %copy.27, s32[1024]{0:T(1024)S(1)} %pad_clamp_fusion.8), kind=kCustom, calls=%fused_computation.8.clone | custom fusion | bytes 2099200 | tf_op jit(solution)/shard_map/jit(_take)/gather | solution.py:44
  55.9 5.2 %multiply_add_fusion = f32[512,1024]{1,0:T(8,128)S(1)} fusion(bf16[512,1024]{1,0:T(8,128)(2,1)} %gather_fusion.7, bf16[512,1024]{1,0:T(8,128)(2,1)} %gather_fusion.6, bf16[512,1024]{1,0:T(8,128)(2,1)} %gather_fusion.5, bf16[512,1024]{1,0:T(8,128)(2,1)} %gather_fusion.4, bf16[512,1024]{1,0:T(8,128)(2,1)} %gather_fusion.3, bf16[512,1024]{1,0:T(8,128)(2,1)} %gather_fusion.2, ...), kind=kLoop, calls=%fused_computation.19 | loop fusion | flops 16252928 | bytes 10506240 | tf_op jit(solution)/shard_map/add | solution.py:45
  63.0 7.1 %multiply_subtract_fusion = (f32[512,2,256]{0,2,1:T(8,128)S(1)}, f32[512,2,256]{0,2,1:T(8,128)S(1)}) fusion(f32[512,2,512]{0,2,1:T(8,128)} %bitcast.65, f32[2,256]{1,0:T(2,128)S(1)} %get-tuple-element.53, f32[512]{0:T(512)S(1)} %bitcast.72, f32[2,256]{1,0:T(2,128)S(1)} %get-tuple-element.54, f32[512]{0:T(512)S(1)} %bitcast.70, ...), kind=kLoop, calls=%fused_computation.29 | loop fusion | flops 2883584 | bytes 4206592 | tf_op jit(solution)/shard_map/sub | solution.py:35
  70.9 33.2 %all-reduce.1 = bf16[512,512]{1,0:T(8,128)(2,1)S(1)} all-reduce(f32[512,512]{1,0:T(8,128)S(1)} %convolution_bitcast_fusion), channel_id=1, replica_groups=mesh['box'=64,'cone'=4] {'cone'}, use_global_device_ids=true, to_apply=%region_0.0 | all-reduce | flops 262144 | bytes 1572864 | tf_op jit(solution)/shard_map/psum | solution.py:82
  104.9 4.6 %subtract_convert_fusion = (bf16[512,2,256]{0,2,1:T(8,128)(2,1)S(1)}, bf16[512,2,256]{0,2,1:T(8,128)(2,1)S(1)}) fusion(f32[512,2,512]{0,2,1:T(8,128)S(1)} %fusion.9, f32[2,256]{1,0:T(2,128)S(1)} %get-tuple-element.53, f32[512]{0:T(512)S(1)} %bitcast.73, f32[2,256]{1,0:T(2,128)S(1)} %get-tuple-element.54, f32[512]{0:T(512)S(1)} %bitcast.71, ...), kind=kLoop, calls=%fused_computation.26 | loop fusion | flops 3670016 | bytes 3158016 | tf_op jit(solution)/shard_map/convert.2
  109.6 1.9 collective-permute-start.2
  111.5 5.8 %collective-permute-start.3 = (bf16[512,2,512]{0,2,1:T(8,128)(2,1)S(1)}, bf16[512,2,512]{0,2,1:T(8,128)(2,1)S(1)}, u32[]{:S(2)}, u32[]{:S(2)}) collective-permute-start(bf16[512,2,512]{0,2,1:T(8,128)(2,1)S(1)} %pad_maximum_fusion.2), channel_id=1, source_target_pairs={{4,0},{8,4},{12,8},{16,12},{20,16},{24,20},{28,24},{32,28},{36,32}... | collective-permute-start | bytes 3145736 | tf_op jit(solution)/shard_map/ppermute | solution.py:15
  117.4 10.4 %collective-permute-done.2 = bf16[512,2,512]{0,2,1:T(8,128)(2,1)S(1)} collective-permute-done((bf16[512,2,512]{0,2,1:T(8,128)(2,1)S(1)}, bf16[512,2,512]{0,2,1:T(8,128)(2,1)S(1)}, u32[]{:S(2)}, u32[]{:S(2)}) %collective-permute-start.2) | collective-permute-done | bytes 1048608 | tf_op jit(solution)/shard_map/ppermute | solution.py:14
  131.4 4.7 %copy.38 = bf16[1536,1024]{1,0:T(8,128)(2,1)} copy(bf16[1536,1024]{0,1:T(8,128)(2,1)} %bitcast.64) | data formatting | bytes 6291456 | tf_op jit(solution)/shard_map/reshape | solution.py:41
  136.0 3.8 %gather_fusion.8 = bf16[256,1024]{1,0:T(8,128)(2,1)S(1)} fusion(bf16[1536,1024]{1,0:T(8,128)(2,1)} %copy.38, s32[1024]{0:T(1024)S(1)} %pad_clamp_fusion.7), kind=kCustom, calls=%fused_computation.1.clone | custom fusion | bytes 1049600 | tf_op jit(solution)/shard_map/jit(_take)/gather | solution.py:44
  139.9 3.9 %gather_fusion.9 = bf16[256,1024]{1,0:T(8,128)(2,1)S(1)} fusion(bf16[1536,1024]{1,0:T(8,128)(2,1)} %copy.38, s32[1024]{0:T(1024)S(1)} %pad_clamp_fusion.6), kind=kCustom, calls=%fused_computation.9.clone | custom fusion | bytes 1049600 | tf_op jit(solution)/shard_map/jit(_take)/gather | solution.py:44
  143.7 4.7 %gather_fusion.10 = bf16[256,1024]{1,0:T(8,128)(2,1)} fusion(bf16[1536,1024]{1,0:T(8,128)(2,1)} %copy.38, s32[1024]{0:T(1024)S(1)} %pad_clamp_fusion.5), kind=kCustom, calls=%fused_computation.10.clone | custom fusion | bytes 1049600 | tf_op jit(solution)/shard_map/jit(_take)/gather | solution.py:44
  148.4 4.6 %gather_fusion.11 = bf16[256,1024]{1,0:T(8,128)(2,1)} fusion(bf16[1536,1024]{1,0:T(8,128)(2,1)} %copy.38, s32[1024]{0:T(1024)S(1)} %pad_clamp_fusion.4), kind=kCustom, calls=%fused_computation.11.clone | custom fusion | bytes 1049600 | tf_op jit(solution)/shard_map/jit(_take)/gather | solution.py:44
  153.0 4.7 %gather_fusion.12 = bf16[256,1024]{1,0:T(8,128)(2,1)} fusion(bf16[1536,1024]{1,0:T(8,128)(2,1)} %copy.38, s32[1024]{0:T(1024)S(1)} %pad_clamp_fusion.3), kind=kCustom, calls=%fused_computation.12.clone | custom fusion | bytes 1049600 | tf_op jit(solution)/shard_map/jit(_take)/gather | solution.py:44
  157.7 4.7 %gather_fusion.13 = bf16[256,1024]{1,0:T(8,128)(2,1)} fusion(bf16[1536,1024]{1,0:T(8,128)(2,1)} %copy.38, s32[1024]{0:T(1024)S(1)} %pad_clamp_fusion.2), kind=kCustom, calls=%fused_computation.13.clone | custom fusion | bytes 1049600 | tf_op jit(solution)/shard_map/jit(_take)/gather | solution.py:44
  162.4 4.6 %gather_fusion.14 = bf16[256,1024]{1,0:T(8,128)(2,1)} fusion(bf16[1536,1024]{1,0:T(8,128)(2,1)} %copy.38, s32[1024]{0:T(1024)S(1)} %pad_clamp_fusion.1), kind=kCustom, calls=%fused_computation.14.clone | custom fusion | bytes 1049600 | tf_op jit(solution)/shard_map/jit(_take)/gather | solution.py:44
  167.0 4.6 %gather_fusion.15 = bf16[256,1024]{1,0:T(8,128)(2,1)} fusion(bf16[1536,1024]{1,0:T(8,128)(2,1)} %copy.38, s32[1024]{0:T(1024)S(1)} %pad_clamp_fusion), kind=kCustom, calls=%fused_computation.15.clone | custom fusion | bytes 1049600 | tf_op jit(solution)/shard_map/jit(_take)/gather | solution.py:44
  171.7 2.7 %multiply_add_fusion.1 = f32[256,1024]{1,0:T(8,128)S(1)} fusion(bf16[256,1024]{1,0:T(8,128)(2,1)} %gather_fusion.15, bf16[256,1024]{1,0:T(8,128)(2,1)} %gather_fusion.14, bf16[256,1024]{1,0:T(8,128)(2,1)} %gather_fusion.13, bf16[256,1024]{1,0:T(8,128)(2,1)} %gather_fusion.12, bf16[256,1024]{1,0:T(8,128)(2,1)} %gather_fusion.11, ...), kind=kLoop, calls=%fused_computation.24 | loop fusion | flops 8126464 | bytes 5253120 | tf_op jit(solution)/shard_map/add | solution.py:45
  175.2 2.5 %subtract_convert_fusion.1 = (bf16[256,2,256]{2,0,1:T(8,128)(2,1)S(1)}, bf16[256,2,256]{2,0,1:T(8,128)(2,1)S(1)}) fusion(f32[256,2,256]{2,0,1:T(8,128)S(1)} %copy.52, f32[256,2,256]{2,0,1:T(8,128)S(1)} %copy.51, f32[2,256]{1,0:T(2,128)S(1)} %get-tuple-element.53, f32[256]{0:T(256)S(1)} %bitcast.111, f32[2,256]{1,0:T(2,128)S(1)} %get-tuple-element.54, ...), kind=kLoop, calls=%fused_computation.41 | loop fusion | flops 1703936 | bytes 1582080 | tf_op jit(solution)/shard_map/convert
  177.8 2.5 %convolution_bitcast_fusion.1 = f32[256,512]{1,0:T(8,128)} fusion(bf16[2,512,512]{2,1,0:T(8,128)(2,1)} %param.21, bf16[256,2,256]{2,0,1:T(8,128)(2,1)S(1)} %get-tuple-element.9, bf16[256,2,256]{2,0,1:T(8,128)(2,1)S(1)} %get-tuple-element.8), kind=kOutput, calls=%fused_computation.22 | convolution fusion | flops 269484032 | bytes 2097152 | tf_op jit(solution)/shard_map/rck,ckn->rn/dot_general | solution.py:90
  181.8 21.3 %reduce-scatter.2.cloned.1.call-done = f32[256,128]{1,0:T(8,128)} async-done(((f32[256,512]{1,0:T(8,128)}), f32[256,128]{1,0:T(8,128)}) %reduce-scatter.2.cloned.1.call-update) | async-done | bytes 131088 | tf_op jit(solution)/shard_map/reduce_scatter | solution.py:93
  (81 shorter events, 20.5 us)
Async XLA Ops:
  7.2 97.0 %copy-start = (bf16[2,512,512]{2,1,0:T(8,128)(2,1)S(1)}, bf16[2,512,512]{2,1,0:T(8,128)(2,1)}, u32[]{:S(2)}) copy-start(bf16[2,512,512]{2,1,0:T(8,128)(2,1)} %param.20) | copy-start | bytes 3145732
  7.2 196.0 %reduce-scatter.2.cloned.1.call-start = ((), (), s32[]{:S(2)}) async-start(), calls=%async_computation.1 | async-start | bytes 655360 | tf_op jit(solution)/shard_map/reduce_scatter | solution.py:93
  8.0 14.3 %copy-start.3 = (s32[8,512]{1,0:T(8,128)S(1)}, s32[8,512]{1,0:T(8,128)}, u32[]{:S(2)}) copy-start(s32[8,512]{1,0:T(8,128)} %param.25) | copy-start | bytes 49156
  8.0 14.5 %copy-start.5 = (s32[8,256]{1,0:T(8,128)S(1)}, s32[8,256]{1,0:T(8,128)}, u32[]{:S(2)}) copy-start(s32[8,256]{1,0:T(8,128)} %param.27) | copy-start | bytes 24580
  8.0 15.7 %copy-start.7 = (s32[2,512]{1,0:T(2,128)S(1)}, s32[2,512]{1,0:T(2,128)}, u32[]{:S(2)}) copy-start(s32[2,512]{1,0:T(2,128)} %param.29) | copy-start | bytes 12292
  8.0 15.7 %copy-start.4 = (f32[8,512]{1,0:T(8,128)S(1)}, f32[8,512]{1,0:T(8,128)}, u32[]{:S(2)}) copy-start(f32[8,512]{1,0:T(8,128)} %param.26) | copy-start | bytes 49156
  13.3 14.0 %collective-permute-start = (bf16[256,2,512]{2,0,1:T(8,128)(2,1)S(1)}, bf16[256,2,512]{2,0,1:T(8,128)(2,1)S(1)}, u32[]{:S(2)}, u32[]{:S(2)}) collective-permute-start(bf16[256,2,512]{2,0,1:T(8,128)(2,1)S(1)} %pad_maximum_fusion.3), channel_id=1, source_target_pairs={{0,4},{4,8},{8,12},{12,16},{16,20},{20,24},{24,28},{28,32},{32,36}... | collective-permute-start | bytes 1572872 | tf_op jit(solution)/shard_map/ppermute | solution.py:14
  15.2 13.9 %collective-permute-start.1 = (bf16[256,2,512]{2,0,1:T(8,128)(2,1)S(1)}, bf16[256,2,512]{2,0,1:T(8,128)(2,1)}, u32[]{:S(2)}, u32[]{:S(2)}) collective-permute-start(bf16[256,2,512]{2,0,1:T(8,128)(2,1)S(1)} %pad_maximum_fusion.3), channel_id=1, source_target_pairs={{4,0},{8,4},{12,8},{16,12},{20,16},{24,20},{28,24},{32,28},{36,32}... | collective-permute-start | bytes 1572872 | tf_op jit(solution)/shard_map/ppermute | solution.py:15
  27.3 0.8 copy-start.2
  63.0 7.1 %copy-start.8 = (bf16[2,512,512]{2,1,0:T(8,128)(2,1)S(1)}, bf16[2,512,512]{2,1,0:T(8,128)(2,1)}, u32[]{:S(2)}) copy-start(bf16[2,512,512]{2,1,0:T(8,128)(2,1)} %param.19) | copy-start | bytes 3145732
  104.1 5.4 %copy-start.1 = (bf16[512,512]{1,0:T(8,128)(2,1)}, bf16[512,512]{1,0:T(8,128)(2,1)S(1)}, u32[]{:S(2)}) copy-start(bf16[512,512]{1,0:T(8,128)(2,1)S(1)} %all-reduce.1) | copy-start | bytes 1572868
  104.9 12.4 %copy-start.6 = (f32[8,256]{1,0:T(8,128)S(1)}, f32[8,256]{1,0:T(8,128)}, u32[]{:S(2)}) copy-start(f32[8,256]{1,0:T(8,128)} %param.28) | copy-start | bytes 24580
  109.6 18.2 %collective-permute-start.2 = (bf16[512,2,512]{0,2,1:T(8,128)(2,1)S(1)}, bf16[512,2,512]{0,2,1:T(8,128)(2,1)S(1)}, u32[]{:S(2)}, u32[]{:S(2)}) collective-permute-start(bf16[512,2,512]{0,2,1:T(8,128)(2,1)S(1)} %pad_maximum_fusion.2), channel_id=1, source_target_pairs={{0,4},{4,8},{8,12},{12,16},{16,20},{20,24},{24,28},{28,32},{32,36}... | collective-permute-start | bytes 3145736 | tf_op jit(solution)/shard_map/ppermute | solution.py:14
  111.5 18.1 %collective-permute-start.3 = (bf16[512,2,512]{0,2,1:T(8,128)(2,1)S(1)}, bf16[512,2,512]{0,2,1:T(8,128)(2,1)S(1)}, u32[]{:S(2)}, u32[]{:S(2)}) collective-permute-start(bf16[512,2,512]{0,2,1:T(8,128)(2,1)S(1)} %pad_maximum_fusion.2), channel_id=1, source_target_pairs={{4,0},{8,4},{12,8},{16,12},{20,16},{24,20},{28,24},{32,28},{36,32}... | collective-permute-start | bytes 3145736 | tf_op jit(solution)/shard_map/ppermute | solution.py:15
Sparse Core Ops, SparseCore 0:
  180.4 22.7 reduce-scatter.1
where the time goes:
time: 211 us; the launch traced here: 210 us
  local copies, waits for them, and re-layouts  73.5 us (35%)
  waiting for transfers between devices  38 us (18%)
  blocking collectives  33.2 us (16%)
  other arithmetic  28.1 us (13%)
  starting transfers between devices  16.8 us (8%)
  between operations  14.7 us (7%)
  matrix products  5.73 us (3%)
    gather x16, local copies, waits for them, and re-layouts, collect(): picked = jnp.take(flat, sources[slot] - offset, axis=0).astype(jnp.float32)  57.9 us
    psum x1, blocking collectives, shards(): po_whole = lax.psum(partial_value, 'cone').astype(jnp.bfloat16)  33.2 us
    reduce_scatter x1, waiting for transfers between devices, shards(): lax.psum_scatter(mom_partial, 'cone', scatter_dimension=1, tiled=True)  21.3 us
    ppermute x2, waiting for transfers between devices, padded_2(): before = lax.ppermute(last, axis, up)  13.9 us
    ppermute x2, starting transfers between devices, padded_2(): after = lax.ppermute(leading, axis, down)  12.9 us
    another operation x3, other arithmetic  9.56 us
    add x2, other arithmetic, collect(): total = total + weights[slot][:, None] * picked  7.95 us
    sub x1, other arithmetic, rotate(): real_part * cosine - imag_part * sine  7.12 us
  transfers between devices with their start and end apart: 5, of which 5 were waited for; matrix products, arithmetic and copies ran while one was open for 1% of the time, Pallas kernels for 0%

commit v1 on v0

--- a/solution.py
+++ b/solution.py
@@ -79,7 +79,7 @@
     partial_value = jnp.einsum(
         "rck,ckn->rn", po_lit, po_receive, preferred_element_type=jnp.float32
     )
-    po_whole = lax.psum(partial_value, "cone").astype(jnp.bfloat16)
+    po_whole = jnp.sum(lax.all_gather(partial_value, "cone"), axis=0).astype(jnp.bfloat16)
     share = po_whole.shape[1] // lax.axis_size("cone")
     po_share = lax.dynamic_slice_in_dim(po_whole, lax.axis_index("cone") * share, share, 1)
     radiated = jnp.einsum("rn,cnk->rck", po_whole, po_radiate, preferred_element_type=jnp.float32)

time: 211 us -> 235 us (1.11)
  waiting for transfers between devices: 38 us -> 91.1 us
  blocking collectives: 33.2 us -> 0 us
  other arithmetic: 28.1 us -> 30.8 us
    all_gather x0 -> x1, waiting for transfers between devices: none -> 51.8 us  [shards(): lax.all_gather(partial_value, 'cone')]
    psum x1 -> x0, blocking collectives: 33.2 us -> none  [shards(): po_whole = lax.psum(partial_value, 'cone').astype(jnp.bfloat16)]
    reduce_sum x0 -> x1, other arithmetic: none -> 2.73 us  [shards(): jnp.sum(lax.all_gather(partial_value, 'cone'), axis=0).astype(jnp.bfloat16)]
  transfers between devices with their start and end apart: 5 -> 6, of which waited for: 5 -> 6; matrix products, arithmetic and copies ran while one was open for 1% -> 1% of each run, Pallas kernels for 0% -> 0%
where the time goes in v1:
time: 235 us; the launch traced here: 234 us
  waiting for transfers between devices  91.1 us (39%)
  local copies, waits for them, and re-layouts  73.4 us (31%)
  other arithmetic  30.8 us (13%)
  starting transfers between devices  17 us (7%)
  between operations  14.7 us (6%)
  matrix products  6.75 us (3%)
    gather x16, local copies, waits for them, and re-layouts, collect(): picked = jnp.take(flat, sources[slot] - offset, axis=0).astype(jnp.float32)  57.8 us
    all_gather x1, waiting for transfers between devices, shards(): lax.all_gather(partial_value, 'cone')  51.8 us
    reduce_scatter x1, waiting for transfers between devices, shards(): lax.psum_scatter(mom_partial, 'cone', scatter_dimension=1, tiled=True)  22.5 us
    ppermute x2, waiting for transfers between devices, padded_2(): before = lax.ppermute(last, axis, up)  14.1 us
    ppermute x2, starting transfers between devices, padded_2(): after = lax.ppermute(leading, axis, down)  12.9 us
    another operation x3, other arithmetic  9.56 us
    add x2, other arithmetic, collect(): total = total + weights[slot][:, None] * picked  7.96 us
    sub x1, other arithmetic, rotate(): real_part * cosine - imag_part * sine  7.12 us
  transfers between devices with their start and end apart: 6, of which 6 were waited for; matrix products, arithmetic and copies ran while one was open for 1% of the time, Pallas kernels for 0%

profile of v1, /device:TPU:2, one launch (start us, length us, event | category | flops | bytes accessed | tf_op | source)
XLA Modules:
  0.0 233.8 jit_solution(3842827183392237135)
XLA Ops:
  10.7 2.5 %subtract_convert_fusion.2 = (bf16[256,2,256]{2,0,1:T(8,128)(2,1)S(1)}, bf16[256,2,256]{2,0,1:T(8,128)(2,1)S(1)}) fusion(f32[256,2,512]{2,0,1:T(8,128)S(1)} %fusion.14, f32[2,256]{1,0:T(2,128)S(1)} %get-tuple-element.53, f32[256]{0:T(256)S(1)} %bitcast.112, f32[2,256]{1,0:T(2,128)S(1)} %get-tuple-element.54, f32[256]{0:T(256)S(1)} %bitcast.110, ...), kind=kLoop, calls=%fused_computation.43 | loop fusion | flops 1835008 | bytes 1582080 | tf_op jit(solution)/shard_map/convert.4
  13.2 1.9 collective-permute-start
  15.2 7.2 %collective-permute-start.1 = (bf16[256,2,512]{2,0,1:T(8,128)(2,1)S(1)}, bf16[256,2,512]{2,0,1:T(8,128)(2,1)}, u32[]{:S(2)}, u32[]{:S(2)}) collective-permute-start(bf16[256,2,512]{2,0,1:T(8,128)(2,1)S(1)} %pad_maximum_fusion.3), channel_id=1, source_target_pairs={{4,0},{8,4},{12,8},{16,12},{20,16},{24,20},{28,24},{32,28},{36,32}... | collective-permute-start | bytes 1572872 | tf_op jit(solution)/shard_map/ppermute | solution.py:15
  23.6 3.7 %collective-permute-done = bf16[256,2,512]{2,0,1:T(8,128)(2,1)S(1)} collective-permute-done((bf16[256,2,512]{2,0,1:T(8,128)(2,1)S(1)}, bf16[256,2,512]{2,0,1:T(8,128)(2,1)S(1)}, u32[]{:S(2)}, u32[]{:S(2)}) %collective-permute-start) | collective-permute-done | bytes 524320 | tf_op jit(solution)/shard_map/ppermute | solution.py:14
  33.7 2.8 %gather_fusion = bf16[512,1024]{1,0:T(8,128)(2,1)} fusion(bf16[768,1024]{1,0:T(8,128)(2,1)S(1)} %copy.27, s32[1024]{0:T(1024)S(1)} %pad_clamp_fusion.15), kind=kCustom, calls=%fused_computation.clone | custom fusion | bytes 2099200 | tf_op jit(solution)/shard_map/jit(_take)/gather | solution.py:44
  36.5 2.7 %gather_fusion.1 = bf16[512,1024]{1,0:T(8,128)(2,1)} fusion(bf16[768,1024]{1,0:T(8,128)(2,1)S(1)} %copy.27, s32[1024]{0:T(1024)S(1)} %pad_clamp_fusion.14), kind=kCustom, calls=%fused_computation.2.clone | custom fusion | bytes 2099200 | tf_op jit(solution)/shard_map/jit(_take)/gather | solution.py:44
  39.2 2.8 %gather_fusion.2 = bf16[512,1024]{1,0:T(8,128)(2,1)} fusion(bf16[768,1024]{1,0:T(8,128)(2,1)S(1)} %copy.27, s32[1024]{0:T(1024)S(1)} %pad_clamp_fusion.13), kind=kCustom, calls=%fused_computation.3.clone | custom fusion | bytes 2099200 | tf_op jit(solution)/shard_map/jit(_take)/gather | solution.py:44
  42.0 2.8 %gather_fusion.3 = bf16[512,1024]{1,0:T(8,128)(2,1)} fusion(bf16[768,1024]{1,0:T(8,128)(2,1)S(1)} %copy.27, s32[1024]{0:T(1024)S(1)} %pad_clamp_fusion.12), kind=kCustom, calls=%fused_computation.4.clone | custom fusion | bytes 2099200 | tf_op jit(solution)/shard_map/jit(_take)/gather | solution.py:44
  44.8 2.8 %gather_fusion.4 = bf16[512,1024]{1,0:T(8,128)(2,1)} fusion(bf16[768,1024]{1,0:T(8,128)(2,1)S(1)} %copy.27, s32[1024]{0:T(1024)S(1)} %pad_clamp_fusion.11), kind=kCustom, calls=%fused_computation.5.clone | custom fusion | bytes 2099200 | tf_op jit(solution)/shard_map/jit(_take)/gather | solution.py:44
  47.6 2.8 %gather_fusion.5 = bf16[512,1024]{1,0:T(8,128)(2,1)} fusion(bf16[768,1024]{1,0:T(8,128)(2,1)S(1)} %copy.27, s32[1024]{0:T(1024)S(1)} %pad_clamp_fusion.10), kind=kCustom, calls=%fused_computation.6.clone | custom fusion | bytes 2099200 | tf_op jit(solution)/shard_map/jit(_take)/gather | solution.py:44
  50.3 2.8 %gather_fusion.6 = bf16[512,1024]{1,0:T(8,128)(2,1)} fusion(bf16[768,1024]{1,0:T(8,128)(2,1)S(1)} %copy.27, s32[1024]{0:T(1024)S(1)} %pad_clamp_fusion.9), kind=kCustom, calls=%fused_computation.7.clone | custom fusion | bytes 2099200 | tf_op jit(solution)/shard_map/jit(_take)/gather | solution.py:44
  53.1 2.8 %gather_fusion.7 = bf16[512,1024]{1,0:T(8,128)(2,1)} fusion(bf16[768,1024]{1,0:T(8,128)(2,1)S(1)} %copy.27, s32[1024]{0:T(1024)S(1)} %pad_clamp_fusion.8), kind=kCustom, calls=%fused_computation.8.clone | custom fusion | bytes 2099200 | tf_op jit(solution)/shard_map/jit(_take)/gather | solution.py:44
  55.9 5.2 %multiply_add_fusion = f32[512,1024]{1,0:T(8,128)S(1)} fusion(bf16[512,1024]{1,0:T(8,128)(2,1)} %gather_fusion.7, bf16[512,1024]{1,0:T(8,128)(2,1)} %gather_fusion.6, bf16[512,1024]{1,0:T(8,128)(2,1)} %gather_fusion.5, bf16[512,1024]{1,0:T(8,128)(2,1)} %gather_fusion.4, bf16[512,1024]{1,0:T(8,128)(2,1)} %gather_fusion.3, bf16[512,1024]{1,0:T(8,128)(2,1)} %gather_fusion.2, ...), kind=kLoop, calls=%fused_computation.19 | loop fusion | flops 16252928 | bytes 10506240 | tf_op jit(solution)/shard_map/add | solution.py:45
  63.0 7.1 %multiply_subtract_fusion = (f32[512,2,256]{0,2,1:T(8,128)S(1)}, f32[512,2,256]{0,2,1:T(8,128)S(1)}) fusion(f32[512,2,512]{0,2,1:T(8,128)} %bitcast.66, f32[2,256]{1,0:T(2,128)S(1)} %get-tuple-element.53, f32[512]{0:T(512)S(1)} %bitcast.74, f32[2,256]{1,0:T(2,128)S(1)} %get-tuple-element.54, f32[512]{0:T(512)S(1)} %bitcast.72, ...), kind=kLoop, calls=%fused_computation.29 | loop fusion | flops 2883584 | bytes 4206592 | tf_op jit(solution)/shard_map/sub | solution.py:35
  72.3 51.8 %all-gather.3.cloned.1.call-done = f32[2048,512]{1,0:T(8,128)} async-done(((f32[512,512]{1,0:T(8,128)}), f32[2048,512]{1,0:T(8,128)}) %all-gather.3.cloned.1.call-update) | async-done | bytes 4194320 | tf_op jit(solution)/shard_map/all_gather | solution.py:82
  124.1 2.7 %reduce_sum.9 = bf16[512,512]{1,0:T(8,128)(2,1)S(1)} reduce(f32[4,512,512]{2,1,0:T(8,128)} %bitcast.68, f32[]{:T(128)} %constant.17.clone.1), dimensions={0}, to_apply=%region_0.0 | reduce | flops 786432 | bytes 4718596 | tf_op jit(solution)/shard_map/reduce_sum | solution.py:82
  127.6 4.6 %subtract_convert_fusion = (bf16[512,2,256]{0,2,1:T(8,128)(2,1)S(1)}, bf16[512,2,256]{0,2,1:T(8,128)(2,1)S(1)}) fusion(f32[512,2,512]{0,2,1:T(8,128)S(1)} %fusion.9, f32[2,256]{1,0:T(2,128)S(1)} %get-tuple-element.53, f32[512]{0:T(512)S(1)} %bitcast.75, f32[2,256]{1,0:T(2,128)S(1)} %get-tuple-element.54, f32[512]{0:T(512)S(1)} %bitcast.73, ...), kind=kLoop, calls=%fused_computation.26 | loop fusion | flops 3670016 | bytes 3158016 | tf_op jit(solution)/shard_map/convert.2
  134.2 5.8 %collective-permute-start.3 = (bf16[512,2,512]{0,2,1:T(8,128)(2,1)S(1)}, bf16[512,2,512]{0,2,1:T(8,128)(2,1)S(1)}, u32[]{:S(2)}, u32[]{:S(2)}) collective-permute-start(bf16[512,2,512]{0,2,1:T(8,128)(2,1)S(1)} %pad_maximum_fusion.2), channel_id=1, source_target_pairs={{4,0},{8,4},{12,8},{16,12},{20,16},{24,20},{28,24},{32,28},{36,32}... | collective-permute-start | bytes 3145736 | tf_op jit(solution)/shard_map/ppermute | solution.py:15
  140.1 10.4 %collective-permute-done.2 = bf16[512,2,512]{0,2,1:T(8,128)(2,1)S(1)} collective-permute-done((bf16[512,2,512]{0,2,1:T(8,128)(2,1)S(1)}, bf16[512,2,512]{0,2,1:T(8,128)(2,1)S(1)}, u32[]{:S(2)}, u32[]{:S(2)}) %collective-permute-start.2) | collective-permute-done | bytes 1048608 | tf_op jit(solution)/shard_map/ppermute | solution.py:14
  154.1 4.6 %copy.38 = bf16[1536,1024]{1,0:T(8,128)(2,1)} copy(bf16[1536,1024]{0,1:T(8,128)(2,1)} %bitcast.65) | data formatting | bytes 6291456 | tf_op jit(solution)/shard_map/reshape | solution.py:41
  158.7 3.8 %gather_fusion.8 = bf16[256,1024]{1,0:T(8,128)(2,1)S(1)} fusion(bf16[1536,1024]{1,0:T(8,128)(2,1)} %copy.38, s32[1024]{0:T(1024)S(1)} %pad_clamp_fusion.7), kind=kCustom, calls=%fused_computation.1.clone | custom fusion | bytes 1049600 | tf_op jit(solution)/shard_map/jit(_take)/gather | solution.py:44
  162.6 3.9 %gather_fusion.9 = bf16[256,1024]{1,0:T(8,128)(2,1)S(1)} fusion(bf16[1536,1024]{1,0:T(8,128)(2,1)} %copy.38, s32[1024]{0:T(1024)S(1)} %pad_clamp_fusion.6), kind=kCustom, calls=%fused_computation.9.clone | custom fusion | bytes 1049600 | tf_op jit(solution)/shard_map/jit(_take)/gather | solution.py:44
  166.4 4.7 %gather_fusion.10 = bf16[256,1024]{1,0:T(8,128)(2,1)} fusion(bf16[1536,1024]{1,0:T(8,128)(2,1)} %copy.38, s32[1024]{0:T(1024)S(1)} %pad_clamp_fusion.5), kind=kCustom, calls=%fused_computation.10.clone | custom fusion | bytes 1049600 | tf_op jit(solution)/shard_map/jit(_take)/gather | solution.py:44
  171.1 4.6 %gather_fusion.11 = bf16[256,1024]{1,0:T(8,128)(2,1)} fusion(bf16[1536,1024]{1,0:T(8,128)(2,1)} %copy.38, s32[1024]{0:T(1024)S(1)} %pad_clamp_fusion.4), kind=kCustom, calls=%fused_computation.11.clone | custom fusion | bytes 1049600 | tf_op jit(solution)/shard_map/jit(_take)/gather | solution.py:44
  175.7 4.7 %gather_fusion.12 = bf16[256,1024]{1,0:T(8,128)(2,1)} fusion(bf16[1536,1024]{1,0:T(8,128)(2,1)} %copy.38, s32[1024]{0:T(1024)S(1)} %pad_clamp_fusion.3), kind=kCustom, calls=%fused_computation.12.clone | custom fusion | bytes 1049600 | tf_op jit(solution)/shard_map/jit(_take)/gather | solution.py:44
  180.4 4.7 %gather_fusion.13 = bf16[256,1024]{1,0:T(8,128)(2,1)} fusion(bf16[1536,1024]{1,0:T(8,128)(2,1)} %copy.38, s32[1024]{0:T(1024)S(1)} %pad_clamp_fusion.2), kind=kCustom, calls=%fused_computation.13.clone | custom fusion | bytes 1049600 | tf_op jit(solution)/shard_map/jit(_take)/gather | solution.py:44
  185.0 4.7 %gather_fusion.14 = bf16[256,1024]{1,0:T(8,128)(2,1)} fusion(bf16[1536,1024]{1,0:T(8,128)(2,1)} %copy.38, s32[1024]{0:T(1024)S(1)} %pad_clamp_fusion.1), kind=kCustom, calls=%fused_computation.14.clone | custom fusion | bytes 1049600 | tf_op jit(solution)/shard_map/jit(_take)/gather | solution.py:44
  189.7 4.6 %gather_fusion.15 = bf16[256,1024]{1,0:T(8,128)(2,1)} fusion(bf16[1536,1024]{1,0:T(8,128)(2,1)} %copy.38, s32[1024]{0:T(1024)S(1)} %pad_clamp_fusion), kind=kCustom, calls=%fused_computation.15.clone | custom fusion | bytes 1049600 | tf_op jit(solution)/shard_map/jit(_take)/gather | solution.py:44
  194.4 2.7 %multiply_add_fusion.1 = f32[256,1024]{1,0:T(8,128)S(1)} fusion(bf16[256,1024]{1,0:T(8,128)(2,1)} %gather_fusion.15, bf16[256,1024]{1,0:T(8,128)(2,1)} %gather_fusion.14, bf16[256,1024]{1,0:T(8,128)(2,1)} %gather_fusion.13, bf16[256,1024]{1,0:T(8,128)(2,1)} %gather_fusion.12, bf16[256,1024]{1,0:T(8,128)(2,1)} %gather_fusion.11, ...), kind=kLoop, calls=%fused_computation.24 | loop fusion | flops 8126464 | bytes 5253120 | tf_op jit(solution)/shard_map/add | solution.py:45
  197.9 2.5 %subtract_convert_fusion.1 = (bf16[256,2,256]{2,0,1:T(8,128)(2,1)S(1)}, bf16[256,2,256]{2,0,1:T(8,128)(2,1)S(1)}) fusion(f32[256,2,256]{2,0,1:T(8,128)S(1)} %copy.52, f32[256,2,256]{2,0,1:T(8,128)S(1)} %copy.51, f32[2,256]{1,0:T(2,128)S(1)} %get-tuple-element.53, f32[256]{0:T(256)S(1)} %bitcast.113, f32[2,256]{1,0:T(2,128)S(1)} %get-tuple-element.54, ...), kind=kLoop, calls=%fused_computation.41 | loop fusion | flops 1703936 | bytes 1582080 | tf_op jit(solution)/shard_map/convert
  200.4 2.5 %convolution_bitcast_fusion.1 = f32[256,512]{1,0:T(8,128)} fusion(bf16[2,512,512]{2,1,0:T(8,128)(2,1)} %param.21, bf16[256,2,256]{2,0,1:T(8,128)(2,1)S(1)} %get-tuple-element.9, bf16[256,2,256]{2,0,1:T(8,128)(2,1)S(1)} %get-tuple-element.8), kind=kOutput, calls=%fused_computation.22 | convolution fusion | flops 269484032 | bytes 2097152 | tf_op jit(solution)/shard_map/rck,ckn->rn/dot_general | solution.py:90
  204.5 22.5 %reduce-scatter.2.cloned.1.call-done = f32[256,128]{1,0:T(8,128)} async-done(((f32[256,512]{1,0:T(8,128)}), f32[256,128]{1,0:T(8,128)}) %reduce-scatter.2.cloned.1.call-update) | async-done | bytes 131088 | tf_op jit(solution)/shard_map/reduce_scatter | solution.py:93
  (84 shorter events, 23.7 us)
Async XLA Ops:
  7.2 119.7 %copy-start = (bf16[2,512,512]{2,1,0:T(8,128)(2,1)S(1)}, bf16[2,512,512]{2,1,0:T(8,128)(2,1)}, u32[]{:S(2)}) copy-start(bf16[2,512,512]{2,1,0:T(8,128)(2,1)} %param.20) | copy-start | bytes 3145732
  7.2 116.9 %all-gather.3.cloned.1.call-start = ((), (), s32[]{:S(2)}) async-start(), calls=%async_computation.2 | async-start | bytes 5242880 | tf_op jit(solution)/shard_map/all_gather | solution.py:82
  8.0 14.3 %copy-start.3 = (s32[8,512]{1,0:T(8,128)S(1)}, s32[8,512]{1,0:T(8,128)}, u32[]{:S(2)}) copy-start(s32[8,512]{1,0:T(8,128)} %param.25) | copy-start | bytes 49156
  8.0 15.5 %copy-start.7 = (s32[2,512]{1,0:T(2,128)S(1)}, s32[2,512]{1,0:T(2,128)}, u32[]{:S(2)}) copy-start(s32[2,512]{1,0:T(2,128)} %param.29) | copy-start | bytes 12292
  8.0 15.5 %copy-start.4 = (f32[8,512]{1,0:T(8,128)S(1)}, f32[8,512]{1,0:T(8,128)}, u32[]{:S(2)}) copy-start(f32[8,512]{1,0:T(8,128)} %param.26) | copy-start | bytes 49156
  13.2 14.0 %collective-permute-start = (bf16[256,2,512]{2,0,1:T(8,128)(2,1)S(1)}, bf16[256,2,512]{2,0,1:T(8,128)(2,1)S(1)}, u32[]{:S(2)}, u32[]{:S(2)}) collective-permute-start(bf16[256,2,512]{2,0,1:T(8,128)(2,1)S(1)} %pad_maximum_fusion.3), channel_id=1, source_target_pairs={{0,4},{4,8},{8,12},{12,16},{16,20},{20,24},{24,28},{28,32},{32,36}... | collective-permute-start | bytes 1572872 | tf_op jit(solution)/shard_map/ppermute | solution.py:14
  15.2 13.9 %collective-permute-start.1 = (bf16[256,2,512]{2,0,1:T(8,128)(2,1)S(1)}, bf16[256,2,512]{2,0,1:T(8,128)(2,1)}, u32[]{:S(2)}, u32[]{:S(2)}) collective-permute-start(bf16[256,2,512]{2,0,1:T(8,128)(2,1)S(1)} %pad_maximum_fusion.3), channel_id=1, source_target_pairs={{4,0},{8,4},{12,8},{16,12},{20,16},{24,20},{28,24},{32,28},{36,32}... | collective-permute-start | bytes 1572872 | tf_op jit(solution)/shard_map/ppermute | solution.py:15
  27.3 0.8 copy-start.2
  63.0 7.1 %copy-start.8 = (bf16[2,512,512]{2,1,0:T(8,128)(2,1)S(1)}, bf16[2,512,512]{2,1,0:T(8,128)(2,1)}, u32[]{:S(2)}) copy-start(bf16[2,512,512]{2,1,0:T(8,128)(2,1)} %param.19) | copy-start | bytes 3145732
  70.1 2.0 copy-start.5
  71.9 155.1 %reduce-scatter.2.cloned.1.call-start = ((), (), s32[]{:S(2)}) async-start(), calls=%async_computation.1 | async-start | bytes 655360 | tf_op jit(solution)/shard_map/reduce_scatter | solution.py:93
  126.9 5.4 %copy-start.1 = (bf16[512,512]{1,0:T(8,128)(2,1)}, bf16[512,512]{1,0:T(8,128)(2,1)S(1)}, u32[]{:S(2)}) copy-start(bf16[512,512]{1,0:T(8,128)(2,1)S(1)} %reduce_sum.9) | copy-start | bytes 1572868
  127.6 12.4 %copy-start.6 = (f32[8,256]{1,0:T(8,128)S(1)}, f32[8,256]{1,0:T(8,128)}, u32[]{:S(2)}) copy-start(f32[8,256]{1,0:T(8,128)} %param.28) | copy-start | bytes 24580
  132.3 18.2 %collective-permute-start.2 = (bf16[512,2,512]{0,2,1:T(8,128)(2,1)S(1)}, bf16[512,2,512]{0,2,1:T(8,128)(2,1)S(1)}, u32[]{:S(2)}, u32[]{:S(2)}) collective-permute-start(bf16[512,2,512]{0,2,1:T(8,128)(2,1)S(1)} %pad_maximum_fusion.2), channel_id=1, source_target_pairs={{0,4},{4,8},{8,12},{12,16},{16,20},{20,24},{24,28},{28,32},{32,36}... | collective-permute-start | bytes 3145736 | tf_op jit(solution)/shard_map/ppermute | solution.py:14
  134.2 18.1 %collective-permute-start.3 = (bf16[512,2,512]{0,2,1:T(8,128)(2,1)S(1)}, bf16[512,2,512]{0,2,1:T(8,128)(2,1)S(1)}, u32[]{:S(2)}, u32[]{:S(2)}) collective-permute-start(bf16[512,2,512]{0,2,1:T(8,128)(2,1)S(1)} %pad_maximum_fusion.2), channel_id=1, source_target_pairs={{4,0},{8,4},{12,8},{16,12},{20,16},{24,20},{28,24},{32,28},{36,32}... | collective-permute-start | bytes 3145736 | tf_op jit(solution)/shard_map/ppermute | solution.py:15
Sparse Core Ops, SparseCore 0:
  72.0 52.0 all-gather.2
  203.0 23.9 reduce-scatter.1
